TPU v7x, 32 devices: a whole 2x2x4 slice. The times are simulated.
32 devices in a mesh: groups: 2 (over y), rows: 8 (over z, core), cols: 2 (over x).
Axes of the slice: x: 2, y: 2, z: 4, core: 2. Of those that a mesh axis runs over, the one named last changes fastest.
Arguments:
- tile_values: bfloat16 [16, 2, 384, 128, 128], P(('groups', 'rows'), 'cols'), parts along dimension 0, may hold values from 0.049804688 to 5
- sketch: bfloat16 [32768, 256], P(('groups', 'rows', 'cols')), parts along dimension 0, may hold values from -6 to 6
- tile_coords: int32 [16, 2, 2, 384], P(('groups', 'rows'), 'cols'), parts along dimension 0, may hold values from 0 to 63, as said below
- tile_counts: int32 [16, 2], P(('groups', 'rows'), 'cols'), parts along dimension 0, may hold values from 1 to 384, as said below
Outputs:
- range_basis: float32 [32768, 256], P(('groups', 'cols', 'rows')), parts along dimension 0
There are 2 independent parts, one for each index of `groups`. A program takes and returns all parts, laid end to end along the dimension named above; each array names one. Nothing has to cross between parts.
Inputs may be any that keep to these rules, and one draw needn't show every extreme that they name: `tile_coords`: the live positions of one device are distinct; every tile on the diagonal of the matrix is live; row numbers are below 64 and column numbers below 16. `tile_counts`: at most 384 live slots a device, reached by some device in every draw.
All inputs are finite; a program needn't handle non-finite values.
Results may differ from a plain program's by a relative error of at most 0.0003.
Values may be sent and summed in bfloat16 or wider, within the bound.
A program may use at most 64 MiB of HBM per device.

v0:
```python
import math

import jax
import jax.numpy as jnp
from jax import lax
from jax.sharding import PartitionSpec as P

TILE_SIZE = 128
SKETCH = 256


def per_device(tile_values, sketch, tile_coords, tile_counts):
    row_count = lax.axis_size("rows")
    col_count = lax.axis_size("cols")
    slot_count = tile_values.shape[2]
    column_block = lax.all_gather(sketch, "cols", axis=0, tiled=True)
    sketch_tiles = column_block.reshape(-1, TILE_SIZE, SKETCH)
    row_tiles = sketch_tiles.shape[0] * row_count // col_count
    slabs = tile_values.reshape(slot_count, TILE_SIZE, TILE_SIZE)
    row_ids = tile_coords[0, 0, 0]
    col_ids = tile_coords[0, 0, 1]
    live = tile_counts[0, 0]
    block_size = math.gcd(slot_count, 32)
    ones_column = jnp.ones((TILE_SIZE,), jnp.bfloat16)

    def visit(number, carry):
        products, totals = carry
        offset = number * block_size
        block_slabs = lax.dynamic_slice_in_dim(slabs, offset, block_size, 0)
        block_rows = lax.dynamic_slice_in_dim(row_ids, offset, block_size, 0)
        block_cols = lax.dynamic_slice_in_dim(col_ids, offset, block_size, 0)
        weight = (offset + jnp.arange(block_size, dtype=jnp.int32) < live).astype(jnp.float32)
        gathered = sketch_tiles[block_cols]
        terms = jnp.einsum(
            "bij,bjk->bik", block_slabs, gathered, preferred_element_type=jnp.float32
        )
        sums = jnp.einsum("bij,j->bi", block_slabs, ones_column, preferred_element_type=jnp.float32)
        products = products.at[block_rows].add(terms * weight[:, None, None])
        totals = totals.at[block_rows].add(sums * weight[:, None])
        return (products, totals)

    block_total = (live + block_size - 1) // block_size
    start = (
        jnp.zeros((row_tiles, TILE_SIZE, SKETCH), jnp.float32),
        jnp.zeros((row_tiles, TILE_SIZE), jnp.float32),
    )
    products, totals = lax.fori_loop(0, block_total, visit, start)
    products = products.reshape(row_tiles * TILE_SIZE, SKETCH)
    totals = totals.reshape(row_tiles * TILE_SIZE)
    contract = (((0,), (0,)), ((), ()))
    products, totals = lax.psum((products, totals), "rows")
    share = products.shape[0] // row_count
    begin = lax.axis_index("rows") * share
    mine = lax.dynamic_slice_in_dim(products, begin, share, 0)
    mine_totals = lax.dynamic_slice_in_dim(totals, begin, share, 0)
    image = mine / mine_totals[:, None]
    gram = lax.psum(
        lax.dot_general(
            image,
            image,
            contract,
            precision=lax.Precision.HIGHEST,
            preferred_element_type=jnp.float32,
        ),
        ("rows", "cols"),
    )
    lower = jnp.linalg.cholesky(gram)
    factor_q = lax.linalg.triangular_solve(
        lower, image, left_side=False, lower=True, transpose_a=True
    )
    states = row_tiles * TILE_SIZE * col_count
    return factor_q * math.sqrt(float(states))


def solution(mesh):
    return jax.shard_map(
        per_device,
        mesh=mesh,
        in_specs=(
            P(("groups", "rows"), "cols", None, None, None),
            P(("groups", "rows", "cols"), None),
            P(("groups", "rows"), "cols", None, None),
            P(("groups", "rows"), "cols"),
        ),
        out_specs=P(("groups", "cols", "rows"), None),
        check_vma=False,
    )
```

profile of v0, /device:TPU:0, one launch (start us, length us, event | category | flops | bytes accessed | tf_op | source)
XLA Modules:
  0.0 591.7 jit_solution(14325621631870415443)
XLA Ops:
  6.5 0.7 all-gather.2.cloned.1.call-update
  8.0 0.8 slice_reduce_fusion
  8.7 24.2 %all-gather.2.cloned.1.call-done = bf16[2048,256]{1,0:T(8,128)(2,1)} async-done(((bf16[1024,256]{1,0:T(8,128)(2,1)}), bf16[2048,256]{1,0:T(8,128)(2,1)}) %all-gather.2.cloned.1.call-update) | async-done | bytes 1048592 | tf_op jit(solution)/shard_map/all_gather | solution.py:16
  32.9 4.2 broadcast_in_dim.21
  37.2 89.2 %while.13 = (s32[]{:T(128)}, f32[64,128,256]{2,1,0:T(8,128)}, f32[64,128]{1,0:T(8,128)S(1)}, s32[]{:T(128)}, s32[384]{0:T(512)S(1)}, /*index=5*/bf16[384,128,128...) while((s32[]{:T(128)}, f32[64,128,256]{2,1,0:T(8,128)}, ...), condition=%wide.region_3.4_spmd, body=%wide.region_0.3_spmd.sunk | while | flops 271590688 | bytes 25237312 | solution.py:47
  37.2 0.1 compare_select_fusion.3
  37.3 0.7 gather_fusion
  38.0 0.7 compare_convert_fusion.2
  38.6 3.9 convolution_multiply_fusion.2
  42.5 10.0 %scatter_fusion = f32[64,128,256]{2,1,0:T(8,128)} fusion(f32[64,128,256]{2,1,0:T(8,128)} %get-tuple-element.207, s32[32]{0:T(128)S(1)} %get-tuple-element.185, f32[32,128,256]{2,1,0:T(8,128)} %convolution_multiply_fusion.2), kind=kCustom, calls=%fused_computation.1.clone.1 | custom fusion | flops 1048576 | bytes 12583040 | tf_op jit(solution)/shard_map/while/body/scatter-add | solution.py:38
  52.5 1.6 fusion.39
  54.1 0.8 scatter_custom_fusion.8
  55.0 0.1 compare_select_fusion.3
  55.1 0.7 gather_fusion
  55.8 0.7 compare_convert_fusion.2
  56.4 3.9 convolution_multiply_fusion.2
  60.3 10.0 %scatter_fusion = f32[64,128,256]{2,1,0:T(8,128)} fusion(f32[64,128,256]{2,1,0:T(8,128)} %get-tuple-element.207, s32[32]{0:T(128)S(1)} %get-tuple-element.185, f32[32,128,256]{2,1,0:T(8,128)} %convolution_multiply_fusion.2), kind=kCustom, calls=%fused_computation.1.clone.1 | custom fusion | flops 1048576 | bytes 12583040 | tf_op jit(solution)/shard_map/while/body/scatter-add | solution.py:38
  70.3 1.6 fusion.39
  71.9 0.8 scatter_custom_fusion.8
  72.8 0.1 compare_select_fusion.3
  72.9 0.7 gather_fusion
  73.6 0.7 compare_convert_fusion.2
  74.2 3.9 convolution_multiply_fusion.2
  78.1 10.0 %scatter_fusion = f32[64,128,256]{2,1,0:T(8,128)} fusion(f32[64,128,256]{2,1,0:T(8,128)} %get-tuple-element.207, s32[32]{0:T(128)S(1)} %get-tuple-element.185, f32[32,128,256]{2,1,0:T(8,128)} %convolution_multiply_fusion.2), kind=kCustom, calls=%fused_computation.1.clone.1 | custom fusion | flops 1048576 | bytes 12583040 | tf_op jit(solution)/shard_map/while/body/scatter-add | solution.py:38
  88.1 1.6 fusion.39
  89.7 0.8 scatter_custom_fusion.8
  90.6 0.1 compare_select_fusion.3
  90.7 0.7 gather_fusion
  91.3 0.7 compare_convert_fusion.2
  92.0 3.9 convolution_multiply_fusion.2
  95.9 10.1 %scatter_fusion = f32[64,128,256]{2,1,0:T(8,128)} fusion(f32[64,128,256]{2,1,0:T(8,128)} %get-tuple-element.207, s32[32]{0:T(128)S(1)} %get-tuple-element.185, f32[32,128,256]{2,1,0:T(8,128)} %convolution_multiply_fusion.2), kind=kCustom, calls=%fused_computation.1.clone.1 | custom fusion | flops 1048576 | bytes 12583040 | tf_op jit(solution)/shard_map/while/body/scatter-add | solution.py:38
  106.0 1.6 fusion.39
  107.6 0.8 scatter_custom_fusion.8
  108.5 0.1 compare_select_fusion.3
  108.6 0.7 gather_fusion
  109.3 0.7 compare_convert_fusion.2
  109.9 3.9 convolution_multiply_fusion.2
  113.8 10.1 %scatter_fusion = f32[64,128,256]{2,1,0:T(8,128)} fusion(f32[64,128,256]{2,1,0:T(8,128)} %get-tuple-element.207, s32[32]{0:T(128)S(1)} %get-tuple-element.185, f32[32,128,256]{2,1,0:T(8,128)} %convolution_multiply_fusion.2), kind=kCustom, calls=%fused_computation.1.clone.1 | custom fusion | flops 1048576 | bytes 12583040 | tf_op jit(solution)/shard_map/while/body/scatter-add | solution.py:38
  124.0 1.6 fusion.39
  125.5 0.8 scatter_custom_fusion.8
  126.5 148.5 %psum.22 = f32[8192]{0:T(1024)S(1)} all-reduce(f32[8192]{0:T(1024)S(1)} %bitcast.50), channel_id=1, replica_groups=mesh['groups'=2,'rows'=8,'cols'=2] {'rows'}, use_global_device_ids=true, to_apply=%region_5.6 | all-reduce | flops 8192 | bytes 65536 | tf_op jit(solution)/shard_map/psum | solution.py:51
  274.9 151.5 %all-reduce.4.cloned.1.call-done = f32[8192,256]{1,0:T(8,128)} async-done(((f32[8192,256]{1,0:T(8,128)}), f32[8192,256]{1,0:T(8,128)}) %all-reduce.4.cloned.1.call-update) | async-done | bytes 8388624 | tf_op jit(solution)/shard_map/psum | solution.py:51
  426.4 1.4 dynamic-slice_divide_fusion
  427.8 2.5 fusion.19
  430.4 89.1 %all-reduce.6.cloned.1.call-done = f32[256,256]{0,1:T(8,128)} async-done(((f32[256,256]{0,1:T(8,128)}), f32[256,256]{0,1:T(8,128)}) %all-reduce.6.cloned.1.call-update) | async-done | bytes 262160 | tf_op jit(solution)/shard_map/psum | solution.py:57
  519.5 1.1 copy.6
  520.5 1.0 fusion.12
  521.6 11.7 %cholesky.50 = f32[128,128]{1,0:T(8,128)S(1)} custom-call(f32[128,128]{1,0:T(8,128)S(1)} %cholesky.118), custom_call_target="Cholesky" | custom-call | tf_op jit(solution)/shard_map/jit(cholesky)/cholesky | solution.py:67
  533.3 9.8 %custom-call.14 = f32[1,128,128]{1,2,0:T(8,128)S(1)} custom-call(f32[1,128,128]{2,1,0:T(8,128)S(1)} %get-tuple-element.99), custom_call_target="InvertDiagBlocksLowerTriangular" | custom-call | tf_op jit(solution)/shard_map/jit(cholesky)/cholesky | solution.py:67
  543.1 0.2 constant_dynamic-update-slice_fusion.1
  543.4 0.3 convolution_subtract_fusion.1
  543.6 11.9 %cholesky.105 = f32[128,128]{1,0:T(8,128)S(1)} custom-call(f32[128,128]{1,0:T(8,128)S(1)} %convolution_subtract_fusion.1), custom_call_target="Cholesky" | custom-call | tf_op jit(solution)/shard_map/jit(cholesky)/cholesky | solution.py:67
  555.5 0.7 compare_reduce_fusion
  557.7 4.1 while.14
  557.7 0.6 fusion.40
  558.3 1.4 bitcast_dynamic-update-slice_fusion.2
  559.8 0.6 fusion.40
  560.3 1.4 bitcast_dynamic-update-slice_fusion.2
  561.8 19.7 %custom-call.15 = f32[2,128,128]{1,2,0:T(8,128)S(1)} custom-call(f32[2,128,128]{2,1,0:T(8,128)S(1)} %get-tuple-element.63), custom_call_target="InvertDiagBlocksLowerTriangular" | custom-call | tf_op jit(solution)/shard_map/triangular_solve | solution.py:68
  581.5 0.6 fusion.10
  582.1 1.0 convolution_subtract_fusion
  583.1 0.6 fusion.13
  583.7 0.1 maximum_multiply_fusion
  583.8 1.3 copy.7
  (24 shorter events, 0.4 us)
Async XLA Ops:
  6.5 26.4 %all-gather.2.cloned.1.call-start = ((), (), s32[]{:S(2)}) async-start(), calls=%async_computation | async-start | bytes 1572864 | tf_op jit(solution)/shard_map/all_gather | solution.py:16
  7.3 419.1 %all-reduce.4.cloned.1.call-start = ((), (), s32[]{:S(2)}) async-start(), calls=%async_computation.1 | async-start | bytes 16777216 | tf_op jit(solution)/shard_map/psum | solution.py:51
  32.9 4.3 copy-start
  126.4 393.0 %all-reduce.6.cloned.1.call-start = ((), (), s32[]{:S(2)}) async-start(), calls=%async_computation.2 | async-start | bytes 524288 | tf_op jit(solution)/shard_map/psum | solution.py:57
Sparse Core Ops, SparseCore 0:
  8.9 23.9 all-gather.1
  126.5 299.8 all-reduce.3
  430.5 88.9 all-reduce.5
where the time goes:
time: 593 us; the launch traced here: 592 us
  waiting for transfers between devices  265 us (45%)
  blocking collectives  148 us (25%)
  other arithmetic  115 us (19%)
  matrix products  32.7 us (6%)
  between operations  15.3 us (3%)
  local copies, waits for them, and re-layouts  15 us (3%)
    psum x1, waiting for transfers between devices, per_device(): products, totals = lax.psum((products, totals), 'rows')  151 us
    psum x1, blocking collectives, per_device(): products, totals = lax.psum((products, totals), 'rows')  148 us
    psum x1, waiting for transfers between devices, per_device(): lax.psum(lax.dot_general(image, image, contract, precision=lax.Precision....  89.1 us
    scatter-add x5, other arithmetic, visit(): products = products.at[block_rows].add(terms * weight[:, None, None])  50.3 us
    another operation x6, other arithmetic, per_device(): lower = jnp.linalg.cholesky(gram)  34.2 us
    all_gather x1, waiting for transfers between devices, per_device(): column_block = lax.all_gather(sketch, 'cols', axis=0, tiled=True)  24.2 us
    another operation x3, other arithmetic, per_device(): lax.linalg.triangular_solve(lower, image, left_side=False, lower=True, tr...  19.7 us
    dot_general x5, matrix products, visit(): jnp.einsum('bij,bjk->bik', block_slabs, gathered, preferred_element_type=...  19.5 us
  transfers between devices with their start and end apart: 3, of which 3 were waited for; matrix products, arithmetic and copies ran while one was open for 0% of the time, Pallas kernels for 0%

commit v1 on v0

v1 whole, which is shorter than its diff:
```python
import functools
import math

import jax
import jax.numpy as jnp
from jax import lax
from jax.experimental import pallas as pl
from jax.experimental.pallas import tpu as pltpu
from jax.sharding import PartitionSpec as P

TILE_SIZE = 128
SKETCH = 256
MESH = pl.DeviceIdType.MESH
CHUNKS = 3
EXTRA = 8
PANEL = 32
HIGHEST = lax.Precision.HIGHEST


def spread(n_rows, n_cols, slots, share, col_tiles, map_ref, tiles_hbm, sketch_hbm, image_ref, gram_ref,
           tiles, block, pair, own, sib_out, sib_in, from_left, from_right,
           tile_sem, local_sem, sk_send, sk_recv, sib_send, sib_recv,
           right_send, right_recv, left_send, left_recv):
    length = n_rows // 2
    part = block.shape[0] // n_cols
    pairs = share // 256
    rows = (share + EXTRA) // CHUNKS
    me = lax.axis_index("rows")
    col = lax.axis_index("cols")
    z = me // 2
    core = lax.rem(me, 2)
    sibling = z * 2 + 1 - core

    tile_copy = pltpu.make_async_copy(tiles_hbm, tiles.at[pl.ds(0, slots)], tile_sem)
    tile_copy.start()
    mine = pl.ds(pl.multiple_of(col * part, part), part)
    sketch_copy = pltpu.make_async_copy(sketch_hbm, block.at[mine], local_sem)
    sketch_copy.start()

    barrier = pltpu.get_barrier_semaphore()
    pl.semaphore_signal(barrier, inc=1, device_id={"rows": sibling}, device_id_type=MESH)
    for step in range(1, n_cols):
        peer = lax.rem(col + step, n_cols)
        pl.semaphore_signal(barrier, inc=1, device_id={"cols": peer}, device_id_type=MESH)

    @pl.when(z > 0)
    def _():
        pl.semaphore_signal(barrier, inc=1, device_id={"rows": me - 2}, device_id_type=MESH)

    @pl.when(z < length - 1)
    def _():
        pl.semaphore_signal(barrier, inc=1, device_id={"rows": me + 2}, device_id_type=MESH)

    near = jnp.where(z > 0, 1, 0) + jnp.where(z < length - 1, 1, 0)
    pl.semaphore_wait(barrier, n_cols + near)

    def sketch_send(step):
        peer = lax.rem(col + step, n_cols)
        return pltpu.make_async_remote_copy(
            src_ref=sketch_hbm, dst_ref=block.at[mine], send_sem=sk_send.at[step], recv_sem=sk_recv.at[step],
            device_id={"cols": peer}, device_id_type=MESH)

    for step in range(1, n_cols):
        sketch_send(step).start()
    tiles[slots] = jnp.zeros((TILE_SIZE, TILE_SIZE), jnp.bfloat16)
    tile_copy.wait()
    sketch_copy.wait()
    for step in range(1, n_cols):
        sketch_send(step).wait()

    ones = jnp.ones((EXTRA, TILE_SIZE), jnp.float32)
    extra_id = lax.broadcasted_iota(jnp.int32, (EXTRA, TILE_SIZE), 0)

    def partial(number, dst, where):
        dst[where, pl.ds(share, EXTRA), :] = jnp.zeros((EXTRA, SKETCH), jnp.float32)

        def one(index, carry):
            for half in range(2):
                base = ((number * pairs + index) * 2 + half) * col_tiles
                total = jnp.zeros((TILE_SIZE, TILE_SIZE), jnp.float32)
                for c in range(col_tiles):
                    slab = tiles[map_ref[base + c]]
                    pair[half * TILE_SIZE:(half + 1) * TILE_SIZE, c * TILE_SIZE:(c + 1) * TILE_SIZE] = slab
                    total = total + slab.astype(jnp.float32)
                sums = lax.dot_general(ones, total, (((1,), (1,)), ((), ())), precision=HIGHEST,
                                       preferred_element_type=jnp.float32)
                lanes = slice(half * TILE_SIZE, (half + 1) * TILE_SIZE)
                kept = dst[where, pl.ds(share, EXTRA), lanes]
                dst[where, pl.ds(share, EXTRA), lanes] = jnp.where(extra_id == index, sums, kept)
            dst[where, pl.ds(pl.multiple_of(index * 256, 256), 256), :] = jnp.dot(
                pair[...], block[...], preferred_element_type=jnp.float32)
            return carry

        lax.fori_loop(0, pairs, one, 0)

    def sib_copy(d):
        return pltpu.make_async_remote_copy(
            src_ref=sib_out.at[d], dst_ref=sib_in.at[d], send_sem=sib_send.at[d], recv_sem=sib_recv.at[d],
            device_id={"rows": sibling}, device_id_type=MESH)

    def right_copy(source, d, c):
        return pltpu.make_async_remote_copy(
            src_ref=source.at[d, pl.ds(c * rows, rows)], dst_ref=from_left.at[d, pl.ds(c * rows, rows)],
            send_sem=right_send.at[d, c], recv_sem=right_recv.at[d, c],
            device_id={"rows": me + 2}, device_id_type=MESH)

    def left_copy(source, d, c):
        return pltpu.make_async_remote_copy(
            src_ref=source.at[d, pl.ds(c * rows, rows)], dst_ref=from_right.at[d, pl.ds(c * rows, rows)],
            send_sem=left_send.at[d, c], recv_sem=left_recv.at[d, c],
            device_id={"rows": me - 2}, device_id_type=MESH)

    def visit(p, carry):
        half = p // 2
        d = jnp.where(lax.rem(p, 2) == 0, length - 1 - half, half)
        partial(d * 2 + 1 - core, sib_out, d)
        sib_copy(d).start()
        partial(d * 2 + core, own, d)
        sib_copy(d).wait()
        own[d] = own[d] + sib_in[d]

        @pl.when((z == 0) & (d > 0))
        def _():
            for c in range(CHUNKS):
                right_copy(own, d, c).start()

        @pl.when((z == length - 1) & (d < z))
        def _():
            for c in range(CHUNKS):
                left_copy(own, d, c).start()

        return carry

    lax.fori_loop(0, length, visit, 0)

    def forward(s, carry):
        d = length - 1 - s
        e = s
        for c in range(CHUNKS):
            span = pl.ds(c * rows, rows)

            @pl.when((z > 0) & (d >= z))
            def _():
                right_copy(from_left, d, c).wait_recv()

                @pl.when(d > z)
                def _():
                    from_left[d, span] = from_left[d, span] + own[d, span]
                    right_copy(from_left, d, c).start()

                @pl.when(d == z)
                def _():
                    own[d, span] = own[d, span] + from_left[d, span]

            @pl.when((z < length - 1) & (e <= z))
            def _():
                left_copy(from_right, e, c).wait_recv()

                @pl.when(e < z)
                def _():
                    from_right[e, span] = from_right[e, span] + own[e, span]
                    left_copy(from_right, e, c).start()

                @pl.when(e == z)
                def _():
                    own[e, span] = own[e, span] + from_right[e, span]

        return carry

    lax.fori_loop(0, length, forward, 0)

    eye = lax.broadcasted_iota(jnp.int32, (256, 256), 0) == lax.broadcasted_iota(jnp.int32, (256, 256), 1)
    gram_ref[...] = jnp.zeros_like(gram_ref)

    def finish(index, carry):
        extra = own[z, pl.ds(share, EXTRA), :]
        picked = lax.broadcasted_iota(jnp.int32, (EXTRA, SKETCH), 0) == index
        line = jnp.sum(jnp.where(picked, extra, 0.0), axis=0, keepdims=True)
        totals = jnp.sum(jnp.where(eye, jnp.broadcast_to(line, (256, 256)), 0.0), axis=1, keepdims=True)
        where = pl.ds(pl.multiple_of(index * 256, 256), 256)
        image = own[z, where, :] / totals
        image_ref[where, :] = image
        gram_ref[...] += lax.dot_general(image, image, (((0,), (0,)), ((), ())), precision=HIGHEST,
                                         preferred_element_type=jnp.float32)
        return carry

    lax.fori_loop(0, pairs, finish, 0)

    def settle(d, carry):
        for c in range(CHUNKS):
            @pl.when((z < length - 1) & (d > z))
            def _():
                right_copy(own, d, c).wait_send()

            @pl.when((z > 0) & (d < z))
            def _():
                left_copy(own, d, c).wait_send()
        return carry

    lax.fori_loop(0, length, settle, 0)


def factor(scale, gram_ref, image_ref, out_ref, work):
    size = SKETCH
    work[:, :size] = gram_ref[...]
    work[:, size:] = (lax.broadcasted_iota(jnp.int32, (size, size), 0)
                      == lax.broadcasted_iota(jnp.int32, (size, size), 1)).astype(jnp.float32)
    row_id = lax.broadcasted_iota(jnp.int32, (PANEL, 1), 0)
    for k in range(size // PANEL):
        first = k * PANEL
        panel = work[first:first + PANEL, :]
        for j in range(PANEL):
            at = first + j
            column = panel[:, at:at + 1]
            inverse = lax.rsqrt(panel[j:j + 1, at:at + 1])
            line = panel[j:j + 1, :] * inverse
            weight = jnp.where(row_id > j, column * inverse, 0.0)
            panel = jnp.where(row_id == j, line, panel - weight * line)
        work[first:first + PANEL, :] = panel
        after = first + PANEL
        if after < size:
            work[after:, :] -= lax.dot_general(
                panel[:, :size], panel, (((0,), (0,)), ((), ())), precision=HIGHEST,
                preferred_element_type=jnp.float32)[after:, :]
    lower = work[:, size:] * scale
    out_ref[...] = lax.dot_general(image_ref[...], lower, (((1,), (1,)), ((), ())), precision=HIGHEST,
                                   preferred_element_type=jnp.float32)


def per_device(tile_values, sketch, tile_coords, tile_counts):
    n_rows = lax.axis_size("rows")
    n_cols = lax.axis_size("cols")
    slots = tile_values.shape[2]
    depth = sketch.shape[0] * n_cols
    col_tiles = depth // TILE_SIZE
    row_tiles = col_tiles * n_rows // n_cols
    share = row_tiles * TILE_SIZE // n_rows
    length = n_rows // 2
    slot = jnp.arange(slots, dtype=jnp.int32)
    place = jnp.where(slot < tile_counts[0, 0], tile_coords[0, 0, 0] * col_tiles + tile_coords[0, 0, 1], -1)
    places = jnp.arange(row_tiles * col_tiles, dtype=jnp.int32)
    where = jnp.min(jnp.where(places[:, None] == place[None, :], slot[None, :], slots), axis=1)
    f32, vmem = jnp.float32, pltpu.VMEM
    dma = pltpu.SemaphoreType.DMA
    image, gram = pl.pallas_call(
        functools.partial(spread, n_rows, n_cols, slots, share, col_tiles),
        out_shape=(jax.ShapeDtypeStruct((share, SKETCH), f32), jax.ShapeDtypeStruct((SKETCH, SKETCH), f32)),
        in_specs=[pl.BlockSpec(memory_space=pltpu.SMEM), pl.BlockSpec(memory_space=pl.ANY),
                  pl.BlockSpec(memory_space=pl.ANY)],
        out_specs=(pl.BlockSpec(memory_space=vmem), pl.BlockSpec(memory_space=vmem)),
        scratch_shapes=[
            vmem((slots + 1, TILE_SIZE, TILE_SIZE), jnp.bfloat16),
            vmem((depth, SKETCH), jnp.bfloat16),
            vmem((256, depth), jnp.bfloat16),
        ] + [vmem((length, share + EXTRA, SKETCH), f32)] * 5 + [
            dma, dma, dma((n_cols,)), dma((n_cols,)), dma((length,)), dma((length,)),
        ] + [dma((length, CHUNKS))] * 4,
        compiler_params=pltpu.CompilerParams(collective_id=0, has_side_effects=True,
                                             vmem_limit_bytes=56 * 1024 * 1024),
    )(where, tile_values.reshape(slots, TILE_SIZE, TILE_SIZE), sketch)
    gram = lax.psum(gram, ("rows", "cols"))
    scale = math.sqrt(float(row_tiles * TILE_SIZE * n_cols))
    return pl.pallas_call(
        functools.partial(factor, scale),
        out_shape=jax.ShapeDtypeStruct((share, SKETCH), f32),
        in_specs=[pl.BlockSpec(memory_space=vmem)] * 2,
        out_specs=pl.BlockSpec(memory_space=vmem),
        scratch_shapes=[vmem((SKETCH, 2 * SKETCH), f32)],
        compiler_params=pltpu.CompilerParams(vmem_limit_bytes=32 * 1024 * 1024),
    )(gram, image)


def solution(mesh):
    return jax.shard_map(
        per_device,
        mesh=mesh,
        in_specs=(
            P(("groups", "rows"), "cols", None, None, None),
            P(("groups", "rows", "cols"), None),
            P(("groups", "rows"), "cols", None, None),
            P(("groups", "rows"), "cols"),
        ),
        out_specs=P(("groups", "cols", "rows"), None),
        check_vma=False,
    )
```

time: 593 us -> 265 us (0.45)
  blocking collectives: 148 us -> 0 us
  waiting for transfers between devices: 265 us -> 119 us
  Pallas kernels: 0 us -> 127 us
  other arithmetic: 115 us -> 1.66 us
  matrix products: 32.7 us -> 0 us
  local copies, waits for them, and re-layouts: 15 us -> 2.17 us
    psum x1 -> x0, blocking collectives: 148 us -> none  [per_device(): products, totals = lax.psum((products, totals), 'rows')]
    pallas_call x0 -> x2, Pallas kernels: none -> 127 us  [the longest x1 100 us: per_device(): pl.pallas_call(functools.partial(spread, n_rows, n_cols, slots, share, co...]
    psum x2 -> x1, waiting for transfers between devices: 241 us -> 119 us  [per_device(): gram = lax.psum(gram, ('rows', 'cols'))]
    scatter-add x10 -> x0, other arithmetic: 54.4 us -> none  [the longest x5 50.3 us: visit(): products = products.at[block_rows].add(terms * weight[:, None, None])]
    another operation x9 -> x0, other arithmetic: 53.9 us -> none  [the longest x6 34.2 us: per_device(): lower = jnp.linalg.cholesky(gram)]
    dot_general x11 -> x0, matrix products: 30 us -> none  [the longest x5 19.5 us: visit(): jnp.einsum('bij,bjk->bik', block_slabs, gathered, preferred_element_type=...]
    all_gather x1 -> x0, waiting for transfers between devices: 24.2 us -> none  [per_device(): column_block = lax.all_gather(sketch, 'cols', axis=0, tiled=True)]
  transfers between devices with their start and end apart: 3 -> 1, of which waited for: 3 -> 1; matrix products, arithmetic and copies ran while one was open for 0% -> 0% of each run, Pallas kernels for 0% -> 0%
where the time goes in v1:
time: 265 us
  Pallas kernels  127 us (48%)
  waiting for transfers between devices  119 us (45%)
  between operations  14.1 us (5%)
    psum x1, waiting for transfers between devices, per_device(): gram = lax.psum(gram, ('rows', 'cols'))  119 us
    pallas_call x1, Pallas kernels, per_device(): pl.pallas_call(functools.partial(spread, n_rows, n_cols, slots, share, co...  100 us
    pallas_call x1, Pallas kernels, per_device(): pl.pallas_call(functools.partial(factor, scale), out_shape=jax.ShapeDtype...  27.1 us
  transfers between devices with their start and end apart: 1, of which 1 were waited for; matrix products, arithmetic and copies ran while one was open for 0% of the time, Pallas kernels for 0%

profile of v1, /device:TPU:0, one launch (start us, length us, event | category | flops | bytes accessed | tf_op | source)
XLA Modules:
  0.0 264.5 jit_solution(15837245358339189156)
XLA Ops:
  6.5 0.0 all-reduce.2.cloned.1.call-start
  7.2 0.8 add_reduce_fusion
  8.0 0.9 select_reduce_fusion.map_ref
  8.9 100.4 %shard_map.46 = (f32[1024,256]{1,0:T(8,128)}, f32[256,256]{1,0:T(8,128)}) custom-call(s32[1024]{0:T(1024)} %select_reduce_fusion.map_ref, bf16[384,128,128]{2,1,0:T(8,128)(2,1)} %bitcast.3, bf16[1024,256]{1,0:T(8,128)(2,1)} %sketch_hbm.1), custom_call_target="tpu_custom_call" | custom-call | tf_op jit(solution)/shard_map/pallas_call | solution.py:245
  109.3 0.0 all-reduce.2.cloned.1.call-update
  109.3 119.1 %all-reduce.2.cloned.1.call-done.gram_ref = f32[256,256]{1,0:T(8,128)} async-done(((f32[256,256]{1,0:T(8,128)}), f32[256,256]{1,0:T(8,128)}) %all-reduce.2.cloned.1.call-update) | async-done | bytes 262160 | tf_op jit(solution)/shard_map/psum | solution.py:261
  228.4 0.0 copy-start
  228.4 1.2 copy-done
  229.6 0.0 copy-start.1
  229.6 0.9 copy-done.1
  230.6 27.1 %shard_map.47 = f32[1024,256]{1,0:T(8,128)} custom-call(f32[256,256]{1,0:T(8,128)S(1)} %copy-done.1, f32[1024,256]{1,0:T(8,128)S(1)} %copy-done), custom_call_target="tpu_custom_call" | custom-call | tf_op jit(solution)/shard_map/pallas_call | solution.py:263
  (1 shorter events, 0.0 us)
Async XLA Ops:
  6.5 221.9 %all-reduce.2.cloned.1.call-start = ((), (), s32[]{:S(2)}) async-start(), calls=%async_computation | async-start | bytes 524288 | tf_op jit(solution)/shard_map/psum | solution.py:261
  228.4 1.2 copy-start
  229.6 0.9 copy-start.1
Sparse Core Ops, SparseCore 0:
  109.4 118.9 all-reduce.1

commit v2 on v1

--- a/solution.py
+++ b/solution.py
@@ -11,20 +11,25 @@
 TILE_SIZE = 128
 SKETCH = 256
 MESH = pl.DeviceIdType.MESH
-CHUNKS = 3
 EXTRA = 8
 PANEL = 32
 HIGHEST = lax.Precision.HIGHEST
 
 
+def aligned(number, unit):
+    return number * unit if isinstance(number, int) else pl.multiple_of(number * unit, unit)
+
+
 def spread(n_rows, n_cols, slots, share, col_tiles, map_ref, tiles_hbm, sketch_hbm, image_ref, gram_ref,
-           tiles, block, pair, own, sib_out, sib_in, from_left, from_right,
+           tiles, block, pair, own, sib_out, sib_in, code_out, code_left, code_right, side_out, side_left, side_right,
+           gram, gram_sib, gram_half, gram_z, gram_cols, gram_all,
            tile_sem, local_sem, sk_send, sk_recv, sib_send, sib_recv,
-           right_send, right_recv, left_send, left_recv):
+           right_send, right_recv, left_send, left_recv,
+           half_sem, sum_send, sum_recv, col_send, col_recv, back_send, back_recv):
     length = n_rows // 2
     part = block.shape[0] // n_cols
     pairs = share // 256
-    rows = (share + EXTRA) // CHUNKS
+    piece = 128 // length
     me = lax.axis_index("rows")
     col = lax.axis_index("cols")
     z = me // 2
@@ -43,16 +48,10 @@
         peer = lax.rem(col + step, n_cols)
         pl.semaphore_signal(barrier, inc=1, device_id={"cols": peer}, device_id_type=MESH)
 
-    @pl.when(z > 0)
-    def _():
-        pl.semaphore_signal(barrier, inc=1, device_id={"rows": me - 2}, device_id_type=MESH)
-
-    @pl.when(z < length - 1)
-    def _():
-        pl.semaphore_signal(barrier, inc=1, device_id={"rows": me + 2}, device_id_type=MESH)
-
-    near = jnp.where(z > 0, 1, 0) + jnp.where(z < length - 1, 1, 0)
-    pl.semaphore_wait(barrier, n_cols + near)
+    for step in range(1, length):
+        peer = lax.rem(z + step, length) * 2 + core
+        pl.semaphore_signal(barrier, inc=1, device_id={"rows": peer}, device_id_type=MESH)
+    pl.semaphore_wait(barrier, n_cols + length - 1)
 
     def sketch_send(step):
         peer = lax.rem(col + step, n_cols)
@@ -98,17 +97,49 @@
             src_ref=sib_out.at[d], dst_ref=sib_in.at[d], send_sem=sib_send.at[d], recv_sem=sib_recv.at[d],
             device_id={"rows": sibling}, device_id_type=MESH)
 
-    def right_copy(source, d, c):
-        return pltpu.make_async_remote_copy(
-            src_ref=source.at[d, pl.ds(c * rows, rows)], dst_ref=from_left.at[d, pl.ds(c * rows, rows)],
-            send_sem=right_send.at[d, c], recv_sem=right_recv.at[d, c],
-            device_id={"rows": me + 2}, device_id_type=MESH)
-
-    def left_copy(source, d, c):
-        return pltpu.make_async_remote_copy(
-            src_ref=source.at[d, pl.ds(c * rows, rows)], dst_ref=from_right.at[d, pl.ds(c * rows, rows)],
-            send_sem=left_send.at[d, c], recv_sem=left_recv.at[d, c],
-            device_id={"rows": me - 2}, device_id_type=MESH)
+    def chain_copies(to_right, d, c):
+        rows, lines = pl.ds(aligned(c, 256), 256), pl.ds(aligned(c, 8), 8)
+        code, side = (code_left, side_left) if to_right else (code_right, side_right)
+        send, recv = (right_send, right_recv) if to_right else (left_send, left_recv)
+        peer = me + 2 if to_right else me - 2
+        return (
+            pltpu.make_async_remote_copy(
+                src_ref=code_out.at[d, rows], dst_ref=code.at[d, rows], send_sem=send.at[d, c, 0],
+                recv_sem=recv.at[d, c, 0], device_id={"rows": peer}, device_id_type=MESH),
+            pltpu.make_async_remote_copy(
+                src_ref=side_out.at[d, lines], dst_ref=side.at[d, lines], send_sem=send.at[d, c, 1],
+                recv_sem=recv.at[d, c, 1], device_id={"rows": peer}, device_id_type=MESH),
+        )
+
+    eye = lax.broadcasted_iota(jnp.int32, (256, 256), 0) == lax.broadcasted_iota(jnp.int32, (256, 256), 1)
+    line_id = lax.broadcasted_iota(jnp.int32, (EXTRA, SKETCH), 0)
+
+    def upright(line):
+        return jnp.sum(jnp.where(eye, jnp.broadcast_to(line, (256, 256)), 0.0), axis=1, keepdims=True)
+
+    def totals_line(d, c):
+        return jnp.sum(jnp.where(line_id == c, own[d, pl.ds(share, EXTRA), :], 0.0), axis=0, keepdims=True)
+
+    def emit(to_right, d, c):
+        rows = pl.ds(aligned(c, 256), 256)
+        line = totals_line(d, c)
+        ratio = own[d, rows, :] / upright(jnp.where(line > 0, line, 1.0))
+        step = jnp.maximum(jnp.max(jnp.abs(ratio), axis=0, keepdims=True) * (1.0 / 32767.0), 1e-30)
+        code_out[d, rows, :] = jnp.round(ratio * (1.0 / step)).astype(jnp.int32).astype(jnp.int16)
+        side_out[d, pl.ds(aligned(c, 8), 8), :] = jnp.where(line_id == 0, line, step)
+        for copy in chain_copies(to_right, d, c):
+            copy.start()
+
+    def absorb(to_right, d, c):
+        for copy in chain_copies(to_right, d, c):
+            copy.wait_recv()
+        code, side = (code_left, side_left) if to_right else (code_right, side_right)
+        rows, extra = pl.ds(aligned(c, 256), 256), pl.ds(share, EXTRA)
+        lines = side[d, pl.ds(aligned(c, 8), 8), :]
+        line, step = lines[0:1], lines[1:2]
+        value = code[d, rows, :].astype(jnp.int32).astype(jnp.float32) * step
+        own[d, rows, :] = own[d, rows, :] + value * upright(line)
+        own[d, extra, :] = own[d, extra, :] + jnp.where(line_id == c, line, 0.0)
 
     def visit(p, carry):
         half = p // 2
@@ -121,83 +152,123 @@
 
         @pl.when((z == 0) & (d > 0))
         def _():
-            for c in range(CHUNKS):
-                right_copy(own, d, c).start()
+            for c in range(pairs):
+                emit(True, d, c)
 
         @pl.when((z == length - 1) & (d < z))
         def _():
-            for c in range(CHUNKS):
-                left_copy(own, d, c).start()
+            for c in range(pairs):
+                emit(False, d, c)
 
         return carry
 
     lax.fori_loop(0, length, visit, 0)
 
-    def forward(s, carry):
-        d = length - 1 - s
-        e = s
-        for c in range(CHUNKS):
-            span = pl.ds(c * rows, rows)
-
-            @pl.when((z > 0) & (d >= z))
+    def forward(index, carry):
+        s, c = index // pairs, lax.rem(index, pairs)
+        d, e = length - 1 - s, s
+
+        @pl.when((z > 0) & (d >= z))
+        def _():
+            absorb(True, d, c)
+
+            @pl.when(d > z)
             def _():
-                right_copy(from_left, d, c).wait_recv()
-
-                @pl.when(d > z)
-                def _():
-                    from_left[d, span] = from_left[d, span] + own[d, span]
-                    right_copy(from_left, d, c).start()
-
-                @pl.when(d == z)
-                def _():
-                    own[d, span] = own[d, span] + from_left[d, span]
-
-            @pl.when((z < length - 1) & (e <= z))
+                emit(True, d, c)
+
+        @pl.when((z < length - 1) & (e <= z))
+        def _():
+            absorb(False, e, c)
+
+            @pl.when(e < z)
             def _():
-                left_copy(from_right, e, c).wait_recv()
-
-                @pl.when(e < z)
-                def _():
-                    from_right[e, span] = from_right[e, span] + own[e, span]
-                    left_copy(from_right, e, c).start()
-
-                @pl.when(e == z)
-                def _():
-                    own[e, span] = own[e, span] + from_right[e, span]
+                emit(False, e, c)
 
         return carry
 
-    lax.fori_loop(0, length, forward, 0)
-
-    eye = lax.broadcasted_iota(jnp.int32, (256, 256), 0) == lax.broadcasted_iota(jnp.int32, (256, 256), 1)
-    gram_ref[...] = jnp.zeros_like(gram_ref)
-
-    def finish(index, carry):
-        extra = own[z, pl.ds(share, EXTRA), :]
-        picked = lax.broadcasted_iota(jnp.int32, (EXTRA, SKETCH), 0) == index
-        line = jnp.sum(jnp.where(picked, extra, 0.0), axis=0, keepdims=True)
-        totals = jnp.sum(jnp.where(eye, jnp.broadcast_to(line, (256, 256)), 0.0), axis=1, keepdims=True)
-        where = pl.ds(pl.multiple_of(index * 256, 256), 256)
-        image = own[z, where, :] / totals
+    lax.fori_loop(0, length * pairs, forward, 0)
+    gram[...] = jnp.zeros_like(gram)
+
+    def finish(c, carry):
+        where = pl.ds(pl.multiple_of(c * 256, 256), 256)
+        image = own[z, where, :] / upright(totals_line(z, c))
         image_ref[where, :] = image
-        gram_ref[...] += lax.dot_general(image, image, (((0,), (0,)), ((), ())), precision=HIGHEST,
-                                         preferred_element_type=jnp.float32)
+        gram[...] += lax.dot_general(image, image, (((0,), (0,)), ((), ())), precision=HIGHEST,
+                                     preferred_element_type=jnp.float32)
         return carry
 
     lax.fori_loop(0, pairs, finish, 0)
 
-    def settle(d, carry):
-        for c in range(CHUNKS):
-            @pl.when((z < length - 1) & (d > z))
-            def _():
-                right_copy(own, d, c).wait_send()
-
-            @pl.when((z > 0) & (d < z))
-            def _():
-                left_copy(own, d, c).wait_send()
+    my_half = pl.ds(pl.multiple_of(core * 128, 128), 128)
+    other_half = pl.ds(pl.multiple_of(128 - core * 128, 128), 128)
+    halves = pltpu.make_async_remote_copy(
+        src_ref=gram.at[other_half], dst_ref=gram_sib, send_sem=half_sem.at[0], recv_sem=half_sem.at[1],
+        device_id={"rows": sibling}, device_id_type=MESH)
+    halves.start()
+    halves.wait()
+    gram_half[...] = gram[my_half, :] + gram_sib[...]
+
+    def piece_of(base, number):
+        return pl.ds(pl.multiple_of(base + number * piece, piece), piece)
+
+    sums = []
+    for step in range(1, length):
+        peer = lax.rem(z + step, length)
+        sums.append(pltpu.make_async_remote_copy(
+            src_ref=gram_half.at[piece_of(0, peer)], dst_ref=gram_z.at[z], send_sem=sum_send.at[step],
+            recv_sem=sum_recv.at[step], device_id={"rows": peer * 2 + core}, device_id_type=MESH))
+        sums[-1].start()
+    total = gram_half[piece_of(0, z), :]
+    for copy in sums:
+        copy.wait()
+    for step in range(1, length):
+        total = total + gram_z[lax.rem(z + step, length)]
+    gram_cols[col] = total
+    crossings = []
+    for step in range(1, n_cols):
+        crossings.append(pltpu.make_async_remote_copy(
+            src_ref=gram_cols.at[col], dst_ref=gram_cols.at[col], send_sem=col_send.at[step],
+            recv_sem=col_recv.at[step], device_id={"cols": lax.rem(col + step, n_cols)}, device_id_type=MESH))
+        crossings[-1].start()
+    for copy in crossings:
+        copy.wait()
+    total = gram_cols[0]
+    for number in range(1, n_cols):
+        total = total + gram_cols[number]
+    place = piece_of(core * 128, z)
+    gram_all[place, :] = total
+    backs = []
+    for step in range(1, length):
+        peer = lax.rem(z + step, length)
+        backs.append(pltpu.make_async_remote_copy(
+            src_ref=gram_all.at[place], dst_ref=gram_all.at[place], send_sem=back_send.at[step],
+            recv_sem=back_recv.at[step], device_id={"rows": peer * 2 + core}, device_id_type=MESH))
+        backs[-1].start()
+    for copy in backs:
+        copy.wait()
+    last = pltpu.make_async_remote_copy(
+        src_ref=gram_all.at[my_half], dst_ref=gram_all.at[my_half], send_sem=half_sem.at[2],
+        recv_sem=half_sem.at[3], device_id={"rows": sibling}, device_id_type=MESH)
+    last.start()
+    last.wait()
+    gram_ref[...] = gram_all[...]
+
+    def settle(index, carry):
+        d, c = index // pairs, lax.rem(index, pairs)
+
+        @pl.when((z < length - 1) & (d > z))
+        def _():
+            for copy in chain_copies(True, d, c):
+                copy.wait_send()
+
+        @pl.when((z > 0) & (d < z))
+        def _():
+            for copy in chain_copies(False, d, c):
+                copy.wait_send()
+
         return carry
 
-    lax.fori_loop(0, length, settle, 0)
+    lax.fori_loop(0, length * pairs, settle, 0)
 
 
 def factor(scale, gram_ref, image_ref, out_ref, work):
@@ -252,13 +323,17 @@
             vmem((slots + 1, TILE_SIZE, TILE_SIZE), jnp.bfloat16),
             vmem((depth, SKETCH), jnp.bfloat16),
             vmem((256, depth), jnp.bfloat16),
-        ] + [vmem((length, share + EXTRA, SKETCH), f32)] * 5 + [
+        ] + [vmem((length, share + EXTRA, SKETCH), f32)] * 3 + [vmem((length, share, SKETCH), jnp.int16)] * 3 + [
+            vmem((length, share // 32, SKETCH), f32)] * 3 + [
+            vmem((SKETCH, SKETCH), f32), vmem((128, SKETCH), f32), vmem((128, SKETCH), f32),
+            vmem((length, 128 // length, SKETCH), f32), vmem((n_cols, 128 // length, SKETCH), f32),
+            vmem((SKETCH, SKETCH), f32),
             dma, dma, dma((n_cols,)), dma((n_cols,)), dma((length,)), dma((length,)),
-        ] + [dma((length, CHUNKS))] * 4,
+        ] + [dma((length, share // 256, 2))] * 4 + [
+            dma((4,)), dma((length,)), dma((length,)), dma((n_cols,)), dma((n_cols,)), dma((length,)), dma((length,))],
         compiler_params=pltpu.CompilerParams(collective_id=0, has_side_effects=True,
                                              vmem_limit_bytes=56 * 1024 * 1024),
     )(where, tile_values.reshape(slots, TILE_SIZE, TILE_SIZE), sketch)
-    gram = lax.psum(gram, ("rows", "cols"))
     scale = math.sqrt(float(row_tiles * TILE_SIZE * n_cols))
     return pl.pallas_call(
         functools.partial(factor, scale),

time: 265 us -> 173 us (0.65)
  waiting for transfers between devices: 119 us -> 0 us
  Pallas kernels: 127 us -> 168 us
  between operations: 14.1 us -> 0.68 us
    psum x1 -> x0, waiting for transfers between devices: 119 us -> none  [per_device(): gram = lax.psum(gram, ('rows', 'cols'))]
    pallas_call x1, Pallas kernels: 100 us -> 141 us  [per_device(): pl.pallas_call(functools.partial(spread, n_rows, n_cols, slots, share, co...]
  transfers between devices with their start and end apart: 1 -> 0, of which waited for: 1 -> 0; matrix products, arithmetic and copies ran while one was open for 0% -> 0% of each run, Pallas kernels for 0% -> 0%
where the time goes in v2:
time: 173 us
  Pallas kernels  168 us (97%)
  local copies, waits for them, and re-layouts  2.17 us (1%)
    pallas_call x1, Pallas kernels, per_device(): pl.pallas_call(functools.partial(spread, n_rows, n_cols, slots, share, co...  141 us
    pallas_call x1, Pallas kernels, per_device(): pl.pallas_call(functools.partial(factor, scale), out_shape=jax.ShapeDtype...  27.1 us

profile of v2, /device:TPU:0, one launch (start us, length us, event | category | flops | bytes accessed | tf_op | source)
XLA Modules:
  0.0 172.9 jit_solution(1992022173259518520)
XLA Ops:
  0.7 0.8 add_reduce_fusion
  1.4 0.9 select_reduce_fusion.map_ref
  2.3 141.3 %shard_map.46 = (f32[1024,256]{1,0:T(8,128)}, f32[256,256]{1,0:T(8,128)}) custom-call(s32[1024]{0:T(1024)} %select_reduce_fusion.map_ref, bf16[384,128,128]{2,1,0:T(8,128)(2,1)} %bitcast.3, bf16[1024,256]{1,0:T(8,128)(2,1)} %sketch_hbm.1), custom_call_target="tpu_custom_call" | custom-call | tf_op jit(solution)/shard_map/pallas_call | solution.py:316
  143.6 0.0 copy-start
  143.6 1.2 copy-done
  144.9 0.0 copy-start.1
  144.9 0.9 copy-done.1
  145.8 27.1 %shard_map.47 = f32[1024,256]{1,0:T(8,128)} custom-call(f32[256,256]{1,0:T(8,128)S(1)} %copy-done.1, f32[1024,256]{1,0:T(8,128)S(1)} %copy-done), custom_call_target="tpu_custom_call" | custom-call | tf_op jit(solution)/shard_map/pallas_call | solution.py:338
  (1 shorter events, 0.0 us)
Async XLA Ops:
  143.6 1.2 copy-start
  144.9 0.9 copy-start.1

commit v3 on v2

--- a/solution.py
+++ b/solution.py
@@ -123,7 +123,7 @@
     def emit(to_right, d, c):
         rows = pl.ds(aligned(c, 256), 256)
         line = totals_line(d, c)
-        ratio = own[d, rows, :] / upright(jnp.where(line > 0, line, 1.0))
+        ratio = own[d, rows, :] * upright(1.0 / jnp.where(line > 0, line, 1.0))
         step = jnp.maximum(jnp.max(jnp.abs(ratio), axis=0, keepdims=True) * (1.0 / 32767.0), 1e-30)
         code_out[d, rows, :] = jnp.round(ratio * (1.0 / step)).astype(jnp.int32).astype(jnp.int16)
         side_out[d, pl.ds(aligned(c, 8), 8), :] = jnp.where(line_id == 0, line, step)
@@ -164,29 +164,41 @@
 
     lax.fori_loop(0, length, visit, 0)
 
+    chunks = length * pairs
+    lag = pairs + 1
+
     def forward(index, carry):
-        s, c = index // pairs, lax.rem(index, pairs)
-        d, e = length - 1 - s, s
-
-        @pl.when((z > 0) & (d >= z))
-        def _():
-            absorb(True, d, c)
-
-            @pl.when(d > z)
+        low = z < length // 2
+        rightward = jnp.where(low, index, index - lag)
+        leftward = jnp.where(low, index - lag, index)
+
+        @pl.when((rightward >= 0) & (rightward < chunks))
+        def _():
+            d, c = length - 1 - rightward // pairs, lax.rem(rightward, pairs)
+
+            @pl.when((z > 0) & (d >= z))
             def _():
-                emit(True, d, c)
-
-        @pl.when((z < length - 1) & (e <= z))
-        def _():
-            absorb(False, e, c)
-
-            @pl.when(e < z)
+                absorb(True, d, c)
+
+                @pl.when(d > z)
+                def _():
+                    emit(True, d, c)
+
+        @pl.when((leftward >= 0) & (leftward < chunks))
+        def _():
+            e, c = leftward // pairs, lax.rem(leftward, pairs)
+
+            @pl.when((z < length - 1) & (e <= z))
             def _():
-                emit(False, e, c)
+                absorb(False, e, c)
+
+                @pl.when(e < z)
+                def _():
+                    emit(False, e, c)
 
         return carry
 
-    lax.fori_loop(0, length * pairs, forward, 0)
+    lax.fori_loop(0, chunks + lag, forward, 0)
     gram[...] = jnp.zeros_like(gram)
 
     def finish(c, carry):
@@ -277,16 +289,23 @@
     work[:, size:] = (lax.broadcasted_iota(jnp.int32, (size, size), 0)
                       == lax.broadcasted_iota(jnp.int32, (size, size), 1)).astype(jnp.float32)
     row_id = lax.broadcasted_iota(jnp.int32, (PANEL, 1), 0)
+    lane_id = lax.broadcasted_iota(jnp.int32, (PANEL, size), 1)
     for k in range(size // PANEL):
         first = k * PANEL
         panel = work[first:first + PANEL, :]
-        for j in range(PANEL):
+        for j in range(0, PANEL, 2):
             at = first + j
-            column = panel[:, at:at + 1]
-            inverse = lax.rsqrt(panel[j:j + 1, at:at + 1])
-            line = panel[j:j + 1, :] * inverse
+            column, second = panel[:, at:at + 1], panel[:, at + 1:at + 2]
+            inverse = 1.0 / column[j:j + 1]
+            ratio = column[j + 1:j + 2] * inverse
+            pivot = second[j + 1:j + 2] - column[j + 1:j + 2] * ratio
+            line = panel[j:j + 1, :]
+            below = panel[j + 1:j + 2, :] - ratio * line
             weight = jnp.where(row_id > j, column * inverse, 0.0)
-            panel = jnp.where(row_id == j, line, panel - weight * line)
+            other = jnp.where(row_id > j + 1, (second - column * ratio) * (1.0 / pivot), 0.0)
+            panel = panel - weight * line - other * below
+        diagonal = jnp.sum(jnp.where(lane_id == first + row_id, panel[:, :size], 0.0), axis=1, keepdims=True)
+        panel = panel * lax.rsqrt(diagonal)
         work[first:first + PANEL, :] = panel
         after = first + PANEL
         if after < size:

time: 173 us -> 126 us (0.73)
  Pallas kernels: 168 us -> 121 us
    pallas_call x1, Pallas kernels: 141 us -> 94 us  [per_device(): pl.pallas_call(functools.partial(spread, n_rows, n_cols, slots, share, co...]
where the time goes in v3:
time: 126 us; the launch traced here: 125 us
  Pallas kernels  121 us (96%)
  local copies, waits for them, and re-layouts  2.17 us (2%)
  other arithmetic  1.66 us (1%)
    pallas_call x1, Pallas kernels, per_device(): pl.pallas_call(functools.partial(spread, n_rows, n_cols, slots, share, co...  94 us
    pallas_call x1, Pallas kernels, per_device(): pl.pallas_call(functools.partial(factor, scale), out_shape=jax.ShapeDtype...  26.8 us

profile of v3, /device:TPU:0, one launch (start us, length us, event | category | flops | bytes accessed | tf_op | source)
XLA Modules:
  0.0 125.3 jit_solution(2147901845838367060)
XLA Ops:
  0.7 0.8 add_reduce_fusion
  1.4 0.9 select_reduce_fusion.map_ref
  2.3 94.0 %shard_map.46 = (f32[1024,256]{1,0:T(8,128)}, f32[256,256]{1,0:T(8,128)}) custom-call(s32[1024]{0:T(1024)} %select_reduce_fusion.map_ref, bf16[384,128,128]{2,1,0:T(8,128)(2,1)} %bitcast.3, bf16[1024,256]{1,0:T(8,128)(2,1)} %sketch_hbm.1), custom_call_target="tpu_custom_call" | custom-call | tf_op jit(solution)/shard_map/pallas_call | solution.py:335
  96.3 0.0 copy-start
  96.4 1.2 copy-done
  97.6 0.0 copy-start.1
  97.6 0.9 copy-done.1
  98.5 26.8 %shard_map.47 = f32[1024,256]{1,0:T(8,128)} custom-call(f32[256,256]{1,0:T(8,128)S(1)} %copy-done.1, f32[1024,256]{1,0:T(8,128)S(1)} %copy-done), custom_call_target="tpu_custom_call" | custom-call | tf_op jit(solution)/shard_map/pallas_call | solution.py:357
  (1 shorter events, 0.0 us)
Async XLA Ops:
  96.3 1.2 copy-start
  97.6 0.9 copy-start.1

commit v4 on v3

--- a/solution.py
+++ b/solution.py
@@ -12,7 +12,7 @@
 SKETCH = 256
 MESH = pl.DeviceIdType.MESH
 EXTRA = 8
-PANEL = 32
+PANEL = 64
 HIGHEST = lax.Precision.HIGHEST
 
 
@@ -309,9 +309,10 @@
         work[first:first + PANEL, :] = panel
         after = first + PANEL
         if after < size:
-            work[after:, :] -= lax.dot_general(
-                panel[:, :size], panel, (((0,), (0,)), ((), ())), precision=HIGHEST,
-                preferred_element_type=jnp.float32)[after:, :]
+            lo, hi = after // 128 * 128, size + (after + 127) // 128 * 128
+            work[after:, lo:hi] -= lax.dot_general(
+                panel[:, lo:size], panel[:, lo:hi], (((0,), (0,)), ((), ())), precision=HIGHEST,
+                preferred_element_type=jnp.float32)[after - lo:, :]
     lower = work[:, size:] * scale
     out_ref[...] = lax.dot_general(image_ref[...], lower, (((1,), (1,)), ((), ())), precision=HIGHEST,
                                    preferred_element_type=jnp.float32)

time: 126 us -> 124 us (0.984)
  Pallas kernels: 121 us -> 119 us
    pallas_call x1, Pallas kernels: 26.8 us -> 24.8 us  [per_device(): pl.pallas_call(functools.partial(factor, scale), out_shape=jax.ShapeDtype...]
where the time goes in v4:
time: 124 us; the launch traced here: 123 us
  Pallas kernels  119 us (96%)
  local copies, waits for them, and re-layouts  2.17 us (2%)
  other arithmetic  1.66 us (1%)
    pallas_call x1, Pallas kernels, per_device(): pl.pallas_call(functools.partial(spread, n_rows, n_cols, slots, share, co...  94.2 us
    pallas_call x1, Pallas kernels, per_device(): pl.pallas_call(functools.partial(factor, scale), out_shape=jax.ShapeDtype...  24.8 us

profile of v4, /device:TPU:0, one launch (start us, length us, event | category | flops | bytes accessed | tf_op | source)
XLA Modules:
  0.0 123.5 jit_solution(4072512721802621442)
XLA Ops:
  0.7 0.8 add_reduce_fusion
  1.4 0.9 select_reduce_fusion.map_ref
  2.3 94.2 %shard_map.46 = (f32[1024,256]{1,0:T(8,128)}, f32[256,256]{1,0:T(8,128)}) custom-call(s32[1024]{0:T(1024)} %select_reduce_fusion.map_ref, bf16[384,128,128]{2,1,0:T(8,128)(2,1)} %bitcast.3, bf16[1024,256]{1,0:T(8,128)(2,1)} %sketch_hbm.1), custom_call_target="tpu_custom_call" | custom-call | tf_op jit(solution)/shard_map/pallas_call | solution.py:336
  96.5 0.0 copy-start
  96.5 1.2 copy-done
  97.7 0.0 copy-start.1
  97.8 0.9 copy-done.1
  98.7 24.8 %shard_map.47 = f32[1024,256]{1,0:T(8,128)} custom-call(f32[256,256]{1,0:T(8,128)S(1)} %copy-done.1, f32[1024,256]{1,0:T(8,128)S(1)} %copy-done), custom_call_target="tpu_custom_call" | custom-call | tf_op jit(solution)/shard_map/pallas_call | solution.py:358
  (1 shorter events, 0.0 us)
Async XLA Ops:
  96.5 1.2 copy-start
  97.7 0.9 copy-start.1
